TPU v7x, 32 devices: a whole 2x2x4 slice. The times are simulated.
32 devices in a mesh: blk: 4 (over x, core), eng: 8 (over z, y).
Axes of the slice: x: 2, y: 2, z: 4, core: 2. Of those that a mesh axis runs over, the one named last changes fastest.
Arguments:
- g_lesser: bfloat16 [32, 4, 2, 256, 256], P('eng', 'blk'), may hold values from -6 to 6
- g_greater: bfloat16 [32, 4, 2, 256, 256], P('eng', 'blk'), may hold values from -6 to 6
- coulomb: bfloat16 [4, 2, 256, 256], P('blk'), may hold values from -0.21875 to 0.21875
- coupling: int32 [4], P('blk'), may hold values 0 or 1
- lag_slots: int32 [32], replicated, may hold values from 0 to 31
Outputs:
- sigma_lesser: bfloat16 [32, 4, 2, 256, 256], P('eng', 'blk')
- sigma_greater: bfloat16 [32, 4, 2, 256, 256], P('eng', 'blk')
Inputs may be any that keep to these rules, and one draw needn't show every extreme that they name: `lag_slots`: offsets may repeat across slots.
All inputs are finite; a program needn't handle non-finite values. No bound on the sum of `coupling` on one device may be relied on, other than what follows from the above.
Results may differ from a plain program's by a relative error of at most 0.0065.
Values may be sent and summed in bfloat16 or wider, within the bound.
A program may use at most 128 MiB of HBM per device.

v0:
```python
import math

import jax
import jax.numpy as jnp
from jax import lax
from jax.sharding import PartitionSpec as P


def padded_2(array, sides, width):
    for axis, dim in sides:
        devices, length = (lax.axis_size(axis), array.shape[dim])
        up = [(i, (i + 1) % devices) for i in range(devices - 1)]
        down = [(j, i) for i, j in up]
        last = lax.slice_in_dim(array, length - width, length, axis=dim)
        leading = lax.slice_in_dim(array, 0, width, axis=dim)
        before = lax.ppermute(last, axis, up)
        after = lax.ppermute(leading, axis, down)
        array = jnp.concatenate([before, array, after], axis=dim)
    return array


def product(einsum_form, left_side, right_side):
    return jnp.einsum(einsum_form, left_side, right_side, preferred_element_type=jnp.float32)


def screen(pad_p, pad_v):
    row_count = pad_v.shape[0] - 2
    v_diag_zero = pad_v[1 : row_count + 1, 0]
    v_diag_plus = pad_v[2:, 0]
    v_up_minus = pad_v[:row_count, 1]
    v_up_zero = pad_v[1 : row_count + 1, 1]
    v_up_plus = pad_v[2:, 1]
    p_diag_minus = pad_p[:, :row_count, 0]
    p_diag_zero = pad_p[:, 1 : row_count + 1, 0]
    p_diag_plus = pad_p[:, 2:, 0]
    p_up_minus = pad_p[:, :row_count, 1]
    p_up_zero = pad_p[:, 1 : row_count + 1, 1]
    p_up_plus = pad_p[:, 2:, 1]
    q_minus = (
        product("rba,krbc->krac", v_up_minus, p_diag_minus)
        + product("rab,krcb->krac", v_diag_zero, p_up_minus)
    ).astype(jnp.bfloat16)
    q_zero = (
        product("rba,krbc->krac", v_up_minus, p_up_minus)
        + product("rab,krbc->krac", v_diag_zero, p_diag_zero)
        + product("rab,krcb->krac", v_up_zero, p_up_zero)
    ).astype(jnp.bfloat16)
    q_plus = (
        product("rab,krbc->krac", v_diag_zero, p_up_zero)
        + product("rab,krbc->krac", v_up_zero, p_diag_plus)
    ).astype(jnp.bfloat16)
    q_far = product("rab,krbc->krac", v_up_zero, p_up_plus).astype(jnp.bfloat16)
    w_diag = (
        product("krab,rbc->krac", q_minus, v_up_minus)
        + product("krab,rbc->krac", q_zero, v_diag_zero)
        + product("krab,rcb->krac", q_plus, v_up_zero)
    )
    w_upper = (
        product("krab,rbc->krac", q_zero, v_up_zero)
        + product("krab,rbc->krac", q_plus, v_diag_plus)
        + product("krab,rcb->krac", q_far, v_up_plus)
    )
    return jnp.stack([w_diag, w_upper], axis=2).astype(jnp.bfloat16)


def tables(row_ids, column_ids, energies):
    phase_ids = row_ids[:, None] * column_ids[None, :] % energies
    angles = phase_ids.astype(jnp.float32) * (2.0 * math.pi / energies)
    return (jnp.cos(angles), jnp.sin(angles))


def matmul(lookup_table, values_in):
    return jnp.dot(
        lookup_table, values_in, precision=lax.Precision.HIGHEST, preferred_element_type=jnp.float32
    )


def correlate_pair(lesser, greater, lag_slots):
    energies = lesser.shape[0]
    layout = lesser.shape
    norm_factor = energies ** (-0.5)
    slot_ids = jnp.arange(energies, dtype=jnp.int32)
    cos_tab, sin_tab = tables(slot_ids, slot_ids, energies)
    cos_lag, sin_lag = tables(lag_slots, slot_ids, energies)
    flat_lesser = lesser.reshape(energies, -1).astype(jnp.float32)
    flat_greater = greater.reshape(energies, -1).astype(jnp.float32)
    lesser_re = matmul(cos_tab, flat_lesser)
    lesser_im = -matmul(sin_tab, flat_lesser)
    greater_re = matmul(cos_tab, flat_greater)
    greater_im = -matmul(sin_tab, flat_greater)
    cross_re = lesser_re * greater_re + lesser_im * greater_im
    cross_im = lesser_im * greater_re - lesser_re * greater_im
    back_re = matmul(cos_lag, cross_re)
    back_im = matmul(sin_lag, cross_im)
    factor = norm_factor / energies
    polar_lesser = ((back_re - back_im) * factor).astype(jnp.bfloat16).reshape(layout)
    polar_greater = ((back_re + back_im) * factor).astype(jnp.bfloat16).reshape(layout)
    return (polar_lesser, polar_greater)


def convolve_pair(green_lesser, green_greater, w_lesser, w_greater, lag_slots):
    energies = green_lesser.shape[0]
    layout = green_lesser.shape
    norm_factor = energies ** (-0.5)
    slot_ids = jnp.arange(energies, dtype=jnp.int32)
    cos_tab, sin_tab = tables(slot_ids, slot_ids, energies)
    cos_lag, sin_lag = tables(slot_ids, lag_slots, energies)

    def convolve_kind(green_part, screened_part):
        flat_green = green_part.reshape(energies, -1).astype(jnp.float32)
        flat_screen = screened_part.reshape(energies, -1).astype(jnp.float32)
        green_re = matmul(cos_tab, flat_green)
        green_im = -matmul(sin_tab, flat_green)
        screen_re = matmul(cos_lag, flat_screen)
        screen_im = -matmul(sin_lag, flat_screen)
        joint_re = green_re * screen_re - green_im * screen_im
        joint_im = green_re * screen_im + green_im * screen_re
        result = matmul(cos_tab, joint_re) - matmul(sin_tab, joint_im)
        return (result * (norm_factor / energies)).astype(jnp.bfloat16).reshape(layout)

    return (convolve_kind(green_lesser, w_lesser), convolve_kind(green_greater, w_greater))


def on_device(g_lesser, g_greater, coulomb, coupling, lag_slots):
    own_energies = g_lesser.shape[0]
    row_count = g_lesser.shape[1]
    el_lesser, el_greater = (
        lax.all_to_all(g_lesser, "eng", split_axis=3, concat_axis=0, tiled=True),
        lax.all_to_all(g_greater, "eng", split_axis=3, concat_axis=0, tiled=True),
    )
    polar_lesser, polar_greater = correlate_pair(el_lesser, el_greater, lag_slots)
    polar_lesser, polar_greater = (
        lax.all_to_all(polar_lesser, "eng", split_axis=0, concat_axis=3, tiled=True),
        lax.all_to_all(polar_greater, "eng", split_axis=0, concat_axis=3, tiled=True),
    )
    row_ids = lax.axis_index("blk") * row_count + jnp.arange(row_count, dtype=jnp.int32)
    all_rows = row_count * lax.axis_size("blk")
    kept_links = (coupling * (row_ids < all_rows - 1).astype(jnp.int32)).astype(jnp.bfloat16)
    v_both = jnp.stack([coulomb[:, 0], coulomb[:, 1] * kept_links[:, None, None]], axis=1)
    stacked = jnp.concatenate([polar_lesser, polar_greater, v_both[None]], axis=0)
    padded = padded_2(stacked, (("blk", 1),), 1)
    screened = screen(padded[: 2 * own_energies], padded[2 * own_energies])
    w_lesser = screened[:own_energies]
    w_greater = screened[own_energies:]
    w_el_lesser, w_el_greater = (
        lax.all_to_all(w_lesser, "eng", split_axis=3, concat_axis=0, tiled=True),
        lax.all_to_all(w_greater, "eng", split_axis=3, concat_axis=0, tiled=True),
    )
    green_lesser, green_greater = (el_lesser, el_greater)
    self_lesser, self_greater = convolve_pair(
        green_lesser, green_greater, w_el_lesser, w_el_greater, lag_slots
    )
    sigma_lesser, sigma_greater = (
        lax.all_to_all(self_lesser, "eng", split_axis=0, concat_axis=3, tiled=True),
        lax.all_to_all(self_greater, "eng", split_axis=0, concat_axis=3, tiled=True),
    )
    return (sigma_lesser, sigma_greater)


def solution(mesh):
    return jax.shard_map(
        on_device,
        mesh=mesh,
        in_specs=(
            P("eng", "blk", None, None, None),
            P("eng", "blk", None, None, None),
            P("blk", None, None, None),
            P("blk"),
            P(),
        ),
        out_specs=(P("eng", "blk", None, None, None), P("eng", "blk", None, None, None)),
        check_vma=False,
    )
```

profile of v0, /device:TPU:1, one launch (start us, length us, event | category | flops | bytes accessed | tf_op | source)
XLA Modules:
  0.0 304.0 jit_solution(14197006566170295009)
XLA Ops:
  0.6 3.1 %copy.87 = bf16[4,1,2,256,256]{4,0,2,1,3:T(4,128)(2,1)} copy(bf16[4,1,2,256,256]{4,3,2,1,0:T(8,128)(2,1)} %param.5) | data formatting | bytes 2097152 | tf_op args[0]
  3.7 6.4 %all-to-all-start = ((bf16[4,1,2,256,256]{4,0,2,1,3:T(4,128)(2,1)}), bf16[4,1,2,256,256]{4,0,2,1,3:T(4,128)(2,1)S(1)}, u32[]{:S(2)}, u32[]{:S(2)}) async-start(bf16[4,1,2,256,256]{4,0,2,1,3:T(4,128)(2,1)} %copy.87), calls=%async_computation | async-start | bytes 2097152 | tf_op jit(solution)/shard_map/all_to_all | solution.py:128
  11.9 22.8 %all-to-all-done = bf16[4,1,2,256,256]{4,0,2,1,3:T(4,128)(2,1)S(1)} async-done(((bf16[4,1,2,256,256]{4,0,2,1,3:T(4,128)(2,1)}), bf16[4,1,2,256,256]{4,0,2,1,3:T(4,128)(2,1)S(1)}, u32[]{:S(2)}, u32[]{:S(2)}) %all-to-all-start) | async-done | bytes 1048608 | tf_op jit(solution)/shard_map/all_to_all | solution.py:128
  34.7 4.9 %all-to-all-start.1 = ((bf16[4,1,2,256,256]{4,0,2,1,3:T(4,128)(2,1)}), bf16[4,1,2,256,256]{4,0,2,1,3:T(4,128)(2,1)S(1)}, u32[]{:S(2)}, u32[]{:S(2)}) async-start(bf16[4,1,2,256,256]{4,0,2,1,3:T(4,128)(2,1)} %copy.89), calls=%async_computation.1 | async-start | bytes 2097152 | tf_op jit(solution)/shard_map/all_to_all | solution.py:129
  40.5 2.4 fusion.86
  42.9 2.4 fusion.80
  45.2 19.5 %all-to-all-done.1 = bf16[4,1,2,256,256]{4,0,2,1,3:T(4,128)(2,1)S(1)} async-done(((bf16[4,1,2,256,256]{4,0,2,1,3:T(4,128)(2,1)}), bf16[4,1,2,256,256]{4,0,2,1,3:T(4,128)(2,1)S(1)}, u32[]{:S(2)}, u32[]{:S(2)}) %all-to-all-start.1) | async-done | bytes 1048608 | tf_op jit(solution)/shard_map/all_to_all | solution.py:129
  70.5 2.3 multiply_convert_fusion.1
  74.0 4.5 %all-to-all-start.3 = ((bf16[32,1,2,32,256]{4,3,2,1,0:T(8,128)(2,1)}), bf16[32,1,2,32,256]{4,3,2,1,0:T(8,128)(2,1)}, u32[]{:S(2)}, u32[]{:S(2)}) async-start(bf16[32,1,2,32,256]{4,3,2,1,0:T(8,128)(2,1)} %bitcast.209), calls=%async_computation.3 | async-start | bytes 2097152 | tf_op jit(solution)/shard_map/all_to_all | solution.py:134
  79.7 23.4 %all-to-all-done.3 = bf16[32,1,2,32,256]{4,3,2,1,0:T(8,128)(2,1)} async-done(((bf16[32,1,2,32,256]{4,3,2,1,0:T(8,128)(2,1)}), bf16[32,1,2,32,256]{4,3,2,1,0:T(8,128)(2,1)}, u32[]{:S(2)}, u32[]{:S(2)}) %all-to-all-start.3) | async-done | bytes 1048608 | tf_op jit(solution)/shard_map/all_to_all | solution.py:134
  103.1 5.0 %all-to-all-start.2 = ((bf16[32,1,2,32,256]{4,3,2,1,0:T(8,128)(2,1)}), bf16[32,1,2,32,256]{4,3,2,1,0:T(8,128)(2,1)}, u32[]{:S(2)}, u32[]{:S(2)}) async-start(bf16[32,1,2,32,256]{4,3,2,1,0:T(8,128)(2,1)} %bitcast.205), calls=%async_computation.2 | async-start | bytes 2097152 | tf_op jit(solution)/shard_map/all_to_all | solution.py:133
  110.2 22.5 %all-to-all-done.2 = bf16[32,1,2,32,256]{4,3,2,1,0:T(8,128)(2,1)} async-done(((bf16[32,1,2,32,256]{4,3,2,1,0:T(8,128)(2,1)}), bf16[32,1,2,32,256]{4,3,2,1,0:T(8,128)(2,1)}, u32[]{:S(2)}, u32[]{:S(2)}) %all-to-all-start.2) | async-done | bytes 1048608 | tf_op jit(solution)/shard_map/all_to_all | solution.py:133
  134.3 4.4 %collective-permute-start.1 = (bf16[9,1,2,256,256]{4,3,2,1,0:T(8,128)(2,1)S(1)}, bf16[9,1,2,256,256]{4,3,2,1,0:T(8,128)(2,1)S(1)}, u32[]{:S(2)}, u32[]{:S(2)}) collective-permute-start(bf16[9,1,2,256,256]{4,3,2,1,0:T(8,128)(2,1)S(1)} %pad_maximum_fusion), channel_id=1, source_target_pairs={{8,0},{16,8},{24,16},{9,1},{17,9},{25,17},{10,2},{18,10},{26,18},{... | collective-permute-start | bytes 7077896 | tf_op jit(solution)/shard_map/ppermute | solution.py:17
  138.7 3.0 collective-permute-start
  141.8 24.6 %collective-permute-done.1 = bf16[9,1,2,256,256]{4,3,2,1,0:T(8,128)(2,1)S(1)} collective-permute-done((bf16[9,1,2,256,256]{4,3,2,1,0:T(8,128)(2,1)S(1)}, bf16[9,1,2,256,256]{4,3,2,1,0:T(8,128)(2,1)S(1)}, u32[]{:S(2)}, u32[]{:S(2)}) %collective-permute-start.1) | collective-permute-done | bytes 2359328 | tf_op jit(solution)/shard_map/ppermute | solution.py:17
  177.3 4.5 %fusion.35 = f32[256,8,256]{2,0,1:T(8,128)} fusion(f32[8,256,256]{2,1,0:T(8,128)} %fusion.45, bf16[9,1,2,256,256]{4,3,2,1,0:T(8,128)(2,1)} %copy-done.6, bf16[3,2,256,256]{3,2,1,0:T(8,128)(2,1)} %copy-done.7), kind=kOutput, calls=%fused_computation.50 | convolution fusion | flops 537919488 | bytes 5505024 | tf_op jit(solution)/shard_map/krab,rbc->krac/dot_general | solution.py:23
  181.9 3.7 %fusion.37 = bf16[8,1,1,256,256]{3,4,0,2,1:T(8,128)(2,1)} fusion(bf16[8,256,256]{1,2,0:T(8,128)(2,1)S(1)} %fusion.34, f32[256,8,256]{2,0,1:T(8,128)} %fusion.35, f32[256,8,256]{2,0,1:T(8,128)} %fusion.52, bf16[3,2,256,256]{3,2,1,0:T(8,128)(2,1)} %copy-done.7), kind=kOutput, calls=%fused_computation.52 | convolution fusion | flops 270008320 | bytes 6422528 | tf_op jit(solution)/shard_map/krab,rcb->krac/dot_general | solution.py:23
  185.5 4.6 %fusion.38 = bf16[8,1,1,256,256]{3,4,0,2,1:T(8,128)(2,1)} fusion(f32[256,8,256]{2,0,1:T(8,128)} %fusion.53, f32[256,8,256]{2,0,1:T(8,128)} %fusion.51, bf16[9,1,2,256,256]{4,3,2,1,0:T(8,128)(2,1)} %copy-done.8, bf16[3,2,256,256]{3,2,1,0:T(8,128)(2,1)} %copy-done.7), kind=kOutput, calls=%fused_computation.53 | convolution fusion | flops 538968064 | bytes 6553600 | tf_op jit(solution)/shard_map/krab,rcb->krac/dot_general | solution.py:23
  190.2 2.7 pad_maximum_fusion.1
  192.9 2.6 copy.111
  195.5 3.6 %all-to-all-start.4 = ((bf16[4,1,2,256,256]{4,0,2,1,3:T(4,128)(2,1)}), bf16[4,1,2,256,256]{4,0,2,1,3:T(4,128)(2,1)S(1)}, u32[]{:S(2)}, u32[]{:S(2)}) async-start(bf16[4,1,2,256,256]{4,0,2,1,3:T(4,128)(2,1)} %copy.111), calls=%async_computation.4 | async-start | bytes 2097152 | tf_op jit(solution)/shard_map/all_to_all | solution.py:146
  199.1 2.6 copy.116
  201.7 22.3 %all-to-all-done.4 = bf16[4,1,2,256,256]{4,0,2,1,3:T(4,128)(2,1)S(1)} async-done(((bf16[4,1,2,256,256]{4,0,2,1,3:T(4,128)(2,1)}), bf16[4,1,2,256,256]{4,0,2,1,3:T(4,128)(2,1)S(1)}, u32[]{:S(2)}, u32[]{:S(2)}) %all-to-all-start.4) | async-done | bytes 1048608 | tf_op jit(solution)/shard_map/all_to_all | solution.py:146
  224.0 4.5 %all-to-all-start.6 = ((bf16[4,1,2,256,256]{4,0,2,1,3:T(4,128)(2,1)}), bf16[4,1,2,256,256]{4,0,2,1,3:T(4,128)(2,1)}, u32[]{:S(2)}, u32[]{:S(2)}) async-start(bf16[4,1,2,256,256]{4,0,2,1,3:T(4,128)(2,1)} %copy.116), calls=%async_computation.6 | async-start | bytes 2097152 | tf_op jit(solution)/shard_map/all_to_all | solution.py:147
  236.1 2.2 fusion.2
  239.5 14.7 %all-to-all-done.6 = bf16[4,1,2,256,256]{4,0,2,1,3:T(4,128)(2,1)} async-done(((bf16[4,1,2,256,256]{4,0,2,1,3:T(4,128)(2,1)}), bf16[4,1,2,256,256]{4,0,2,1,3:T(4,128)(2,1)}, u32[]{:S(2)}, u32[]{:S(2)}) %all-to-all-start.6) | async-done | bytes 1048608 | tf_op jit(solution)/shard_map/all_to_all | solution.py:147
  254.2 4.5 %all-to-all-start.5 = ((bf16[32,1,2,32,256]{4,3,2,1,0:T(8,128)(2,1)}), bf16[32,1,2,32,256]{4,3,2,1,0:T(8,128)(2,1)}, u32[]{:S(2)}, u32[]{:S(2)}) async-start(bf16[32,1,2,32,256]{4,3,2,1,0:T(8,128)(2,1)} %bitcast.64), calls=%async_computation.5 | async-start | bytes 2097152 | tf_op jit(solution)/shard_map/all_to_all | solution.py:154
  267.5 2.3 fusion.3
  271.0 12.9 %all-to-all-done.5 = bf16[32,1,2,32,256]{4,3,2,1,0:T(8,128)(2,1)} async-done(((bf16[32,1,2,32,256]{4,3,2,1,0:T(8,128)(2,1)}), bf16[32,1,2,32,256]{4,3,2,1,0:T(8,128)(2,1)}, u32[]{:S(2)}, u32[]{:S(2)}) %all-to-all-start.5) | async-done | bytes 1048608 | tf_op jit(solution)/shard_map/all_to_all | solution.py:154
  284.0 3.9 %all-to-all-start.7 = ((bf16[32,1,2,32,256]{4,3,2,1,0:T(8,128)(2,1)}), bf16[32,1,2,32,256]{4,3,2,1,0:T(8,128)(2,1)S(1)}, u32[]{:S(2)}, u32[]{:S(2)}) async-start(bf16[32,1,2,32,256]{4,3,2,1,0:T(8,128)(2,1)} %bitcast.70), calls=%async_computation.7 | async-start | bytes 2097152 | tf_op jit(solution)/shard_map/all_to_all | solution.py:155
  287.9 2.3 copy.115
  290.2 12.7 %all-to-all-done.7 = bf16[32,1,2,32,256]{4,3,2,1,0:T(8,128)(2,1)S(1)} async-done(((bf16[32,1,2,32,256]{4,3,2,1,0:T(8,128)(2,1)}), bf16[32,1,2,32,256]{4,3,2,1,0:T(8,128)(2,1)S(1)}, u32[]{:S(2)}, u32[]{:S(2)}) %all-to-all-start.7) | async-done | bytes 1048608 | tf_op jit(solution)/shard_map/all_to_all | solution.py:155
  (67 shorter events, 44.4 us)
Async XLA Ops:
  0.6 9.5 %copy-start.10 = (bf16[4,1,2,256,256]{4,3,2,1,0:T(8,128)(2,1)S(1)}, bf16[4,1,2,256,256]{4,3,2,1,0:T(8,128)(2,1)}, u32[]{:S(2)}) copy-start(bf16[4,1,2,256,256]{4,3,2,1,0:T(8,128)(2,1)} %param.6) | copy-start | bytes 3145732
  3.7 31.0 %all-to-all-start = ((bf16[4,1,2,256,256]{4,0,2,1,3:T(4,128)(2,1)}), bf16[4,1,2,256,256]{4,0,2,1,3:T(4,128)(2,1)S(1)}, u32[]{:S(2)}, u32[]{:S(2)}) async-start(bf16[4,1,2,256,256]{4,0,2,1,3:T(4,128)(2,1)} %copy.87), calls=%async_computation | async-start | bytes 2097152 | tf_op jit(solution)/shard_map/all_to_all | solution.py:128
  34.7 30.0 %all-to-all-start.1 = ((bf16[4,1,2,256,256]{4,0,2,1,3:T(4,128)(2,1)}), bf16[4,1,2,256,256]{4,0,2,1,3:T(4,128)(2,1)S(1)}, u32[]{:S(2)}, u32[]{:S(2)}) async-start(bf16[4,1,2,256,256]{4,0,2,1,3:T(4,128)(2,1)} %copy.89), calls=%async_computation.1 | async-start | bytes 2097152 | tf_op jit(solution)/shard_map/all_to_all | solution.py:129
  65.6 2.1 copy-start.4
  66.6 1.7 copy-start.2
  66.6 1.7 copy-start.12
  68.4 2.1 copy-start
  74.0 29.1 %all-to-all-start.3 = ((bf16[32,1,2,32,256]{4,3,2,1,0:T(8,128)(2,1)}), bf16[32,1,2,32,256]{4,3,2,1,0:T(8,128)(2,1)}, u32[]{:S(2)}, u32[]{:S(2)}) async-start(bf16[32,1,2,32,256]{4,3,2,1,0:T(8,128)(2,1)} %bitcast.209), calls=%async_computation.3 | async-start | bytes 2097152 | tf_op jit(solution)/shard_map/all_to_all | solution.py:134
  78.5 30.3 %copy-start.11 = (bf16[1,2,256,256]{3,2,1,0:T(8,128)(2,1)S(1)}, bf16[1,2,256,256]{3,2,1,0:T(8,128)(2,1)}, u32[]{:S(2)}) copy-start(bf16[1,2,256,256]{3,2,1,0:T(8,128)(2,1)} %param.7) | copy-start | bytes 786436
  103.1 29.6 %all-to-all-start.2 = ((bf16[32,1,2,32,256]{4,3,2,1,0:T(8,128)(2,1)}), bf16[32,1,2,32,256]{4,3,2,1,0:T(8,128)(2,1)}, u32[]{:S(2)}, u32[]{:S(2)}) async-start(bf16[32,1,2,32,256]{4,3,2,1,0:T(8,128)(2,1)} %bitcast.205), calls=%async_computation.2 | async-start | bytes 2097152 | tf_op jit(solution)/shard_map/all_to_all | solution.py:133
  134.3 32.0 %collective-permute-start.1 = (bf16[9,1,2,256,256]{4,3,2,1,0:T(8,128)(2,1)S(1)}, bf16[9,1,2,256,256]{4,3,2,1,0:T(8,128)(2,1)S(1)}, u32[]{:S(2)}, u32[]{:S(2)}) collective-permute-start(bf16[9,1,2,256,256]{4,3,2,1,0:T(8,128)(2,1)S(1)} %pad_maximum_fusion), channel_id=1, source_target_pairs={{8,0},{16,8},{24,16},{9,1},{17,9},{25,17},{10,2},{18,10},{26,18},{... | collective-permute-start | bytes 7077896 | tf_op jit(solution)/shard_map/ppermute | solution.py:17
  138.7 28.8 %collective-permute-start = (bf16[9,1,2,256,256]{4,3,2,1,0:T(8,128)(2,1)S(1)}, bf16[9,1,2,256,256]{4,3,2,1,0:T(8,128)(2,1)S(1)}, u32[]{:S(2)}, u32[]{:S(2)}) collective-permute-start(bf16[9,1,2,256,256]{4,3,2,1,0:T(8,128)(2,1)S(1)} %pad_maximum_fusion), channel_id=1, source_target_pairs={{0,8},{8,16},{16,24},{1,9},{9,17},{17,25},{2,10},{10,18},{18,26},{... | collective-permute-start | bytes 7077896 | tf_op jit(solution)/shard_map/ppermute | solution.py:16
  166.3 6.9 %copy-start.8 = (bf16[9,1,2,256,256]{4,3,2,1,0:T(8,128)(2,1)}, bf16[9,1,2,256,256]{4,3,2,1,0:T(8,128)(2,1)S(1)}, u32[]{:S(2)}) copy-start(bf16[9,1,2,256,256]{4,3,2,1,0:T(8,128)(2,1)S(1)} %collective-permute-done.1) | copy-start | bytes 7077892
  167.5 8.0 %copy-start.6 = (bf16[9,1,2,256,256]{4,3,2,1,0:T(8,128)(2,1)}, bf16[9,1,2,256,256]{4,3,2,1,0:T(8,128)(2,1)S(1)}, u32[]{:S(2)}) copy-start(bf16[9,1,2,256,256]{4,3,2,1,0:T(8,128)(2,1)S(1)} %collective-permute-done) | copy-start | bytes 7077892
  167.6 7.9 %copy-start.7 = (bf16[3,2,256,256]{3,2,1,0:T(8,128)(2,1)}, bf16[3,2,256,256]{3,2,1,0:T(8,128)(2,1)S(1)}, u32[]{:S(2)}) copy-start(bf16[3,2,256,256]{3,2,1,0:T(8,128)(2,1)S(1)} %fusion.46) | copy-start | bytes 2359300
  185.5 4.6 %copy-start.9 = (bf16[8,1,1,256,256]{3,4,0,2,1:T(8,128)(2,1)S(1)}, bf16[8,1,1,256,256]{3,4,0,2,1:T(8,128)(2,1)}, u32[]{:S(2)}) copy-start(bf16[8,1,1,256,256]{3,4,0,2,1:T(8,128)(2,1)} %fusion.37) | copy-start | bytes 3145732
  195.5 28.5 %all-to-all-start.4 = ((bf16[4,1,2,256,256]{4,0,2,1,3:T(4,128)(2,1)}), bf16[4,1,2,256,256]{4,0,2,1,3:T(4,128)(2,1)S(1)}, u32[]{:S(2)}, u32[]{:S(2)}) async-start(bf16[4,1,2,256,256]{4,0,2,1,3:T(4,128)(2,1)} %copy.111), calls=%async_computation.4 | async-start | bytes 2097152 | tf_op jit(solution)/shard_map/all_to_all | solution.py:146
  224.0 30.2 %all-to-all-start.6 = ((bf16[4,1,2,256,256]{4,0,2,1,3:T(4,128)(2,1)}), bf16[4,1,2,256,256]{4,0,2,1,3:T(4,128)(2,1)}, u32[]{:S(2)}, u32[]{:S(2)}) async-start(bf16[4,1,2,256,256]{4,0,2,1,3:T(4,128)(2,1)} %copy.116), calls=%async_computation.6 | async-start | bytes 2097152 | tf_op jit(solution)/shard_map/all_to_all | solution.py:147
  231.3 2.1 copy-start.5
  232.3 1.7 copy-start.3
  254.2 29.8 %all-to-all-start.5 = ((bf16[32,1,2,32,256]{4,3,2,1,0:T(8,128)(2,1)}), bf16[32,1,2,32,256]{4,3,2,1,0:T(8,128)(2,1)}, u32[]{:S(2)}, u32[]{:S(2)}) async-start(bf16[32,1,2,32,256]{4,3,2,1,0:T(8,128)(2,1)} %bitcast.64), calls=%async_computation.5 | async-start | bytes 2097152 | tf_op jit(solution)/shard_map/all_to_all | solution.py:154
  263.8 1.6 copy-start.1
  284.0 18.9 %all-to-all-start.7 = ((bf16[32,1,2,32,256]{4,3,2,1,0:T(8,128)(2,1)}), bf16[32,1,2,32,256]{4,3,2,1,0:T(8,128)(2,1)S(1)}, u32[]{:S(2)}, u32[]{:S(2)}) async-start(bf16[32,1,2,32,256]{4,3,2,1,0:T(8,128)(2,1)} %bitcast.70), calls=%async_computation.7 | async-start | bytes 2097152 | tf_op jit(solution)/shard_map/all_to_all | solution.py:155
where the time goes:
time: 305 us; the launch traced here: 304 us
  waiting for transfers between devices  177 us (58%)
  matrix products  46.6 us (15%)
  starting transfers between devices  44.7 us (15%)
  local copies, waits for them, and re-layouts  31.3 us (10%)
  other arithmetic  3.13 us (1%)
    ppermute x1, waiting for transfers between devices, padded_2(): after = lax.ppermute(leading, axis, down)  24.6 us
    dot_general x14, matrix products, matmul(): jnp.dot(lookup_table, values_in, precision=lax.Precision.HIGHEST, preferr...  24.1 us
    all_to_all x1, waiting for transfers between devices, on_device(): lax.all_to_all(polar_greater, 'eng', split_axis=0, concat_axis=3, tiled=T...  23.4 us
    all_to_all x1, waiting for transfers between devices, on_device(): lax.all_to_all(g_lesser, 'eng', split_axis=3, concat_axis=0, tiled=True)  22.8 us
    all_to_all x1, waiting for transfers between devices, on_device(): lax.all_to_all(polar_lesser, 'eng', split_axis=0, concat_axis=3, tiled=True)  22.5 us
    dot_general x12, matrix products, product(): jnp.einsum(einsum_form, left_side, right_side, preferred_element_type=jnp...  22.5 us
    all_to_all x1, waiting for transfers between devices, on_device(): lax.all_to_all(w_lesser, 'eng', split_axis=3, concat_axis=0, tiled=True)  22.3 us
    all_to_all x1, waiting for transfers between devices, on_device(): lax.all_to_all(g_greater, 'eng', split_axis=3, concat_axis=0, tiled=True)  19.5 us
  transfers between devices with their start and end apart: 10, of which 10 were waited for; matrix products, arithmetic and copies ran while one was open for 12% of the time, Pallas kernels for 0%

commit v1 on v0

--- a/solution.py
+++ b/solution.py
@@ -75,13 +75,11 @@
     )
 
 
-def correlate_pair(lesser, greater, lag_slots):
+def correlate(lesser, greater):
     energies = lesser.shape[0]
     layout = lesser.shape
-    norm_factor = energies ** (-0.5)
     slot_ids = jnp.arange(energies, dtype=jnp.int32)
     cos_tab, sin_tab = tables(slot_ids, slot_ids, energies)
-    cos_lag, sin_lag = tables(lag_slots, slot_ids, energies)
     flat_lesser = lesser.reshape(energies, -1).astype(jnp.float32)
     flat_greater = greater.reshape(energies, -1).astype(jnp.float32)
     lesser_re = matmul(cos_tab, flat_lesser)
@@ -90,35 +88,31 @@
     greater_im = -matmul(sin_tab, flat_greater)
     cross_re = lesser_re * greater_re + lesser_im * greater_im
     cross_im = lesser_im * greater_re - lesser_re * greater_im
-    back_re = matmul(cos_lag, cross_re)
-    back_im = matmul(sin_lag, cross_im)
-    factor = norm_factor / energies
-    polar_lesser = ((back_re - back_im) * factor).astype(jnp.bfloat16).reshape(layout)
-    polar_greater = ((back_re + back_im) * factor).astype(jnp.bfloat16).reshape(layout)
-    return (polar_lesser, polar_greater)
+    back = matmul(cos_tab, cross_re) - matmul(sin_tab, cross_im)
+    return (back * (energies ** (-1.5))).astype(jnp.bfloat16).reshape(layout)
 
 
-def convolve_pair(green_lesser, green_greater, w_lesser, w_greater, lag_slots):
+def convolve_pair(green_lesser, green_greater, screened, lag_slots):
     energies = green_lesser.shape[0]
     layout = green_lesser.shape
-    norm_factor = energies ** (-0.5)
     slot_ids = jnp.arange(energies, dtype=jnp.int32)
     cos_tab, sin_tab = tables(slot_ids, slot_ids, energies)
-    cos_lag, sin_lag = tables(slot_ids, lag_slots, energies)
+    hits = jnp.sum((lag_slots[:, None] == slot_ids[None, :]).astype(jnp.float32), axis=0)
+    mirrored = jnp.roll(hits[::-1], 1)
+    flat_screen = screened.reshape(energies, -1).astype(jnp.float32)
 
-    def convolve_kind(green_part, screened_part):
+    def convolve_kind(green_part, weights, sign):
         flat_green = green_part.reshape(energies, -1).astype(jnp.float32)
-        flat_screen = screened_part.reshape(energies, -1).astype(jnp.float32)
         green_re = matmul(cos_tab, flat_green)
         green_im = -matmul(sin_tab, flat_green)
-        screen_re = matmul(cos_lag, flat_screen)
-        screen_im = -matmul(sin_lag, flat_screen)
+        screen_re = matmul(cos_tab * weights[None, :], flat_screen)
+        screen_im = -sign * matmul(sin_tab * weights[None, :], flat_screen)
         joint_re = green_re * screen_re - green_im * screen_im
         joint_im = green_re * screen_im + green_im * screen_re
         result = matmul(cos_tab, joint_re) - matmul(sin_tab, joint_im)
-        return (result * (norm_factor / energies)).astype(jnp.bfloat16).reshape(layout)
+        return (result * (energies ** (-1.5))).astype(jnp.bfloat16).reshape(layout)
 
-    return (convolve_kind(green_lesser, w_lesser), convolve_kind(green_greater, w_greater))
+    return (convolve_kind(green_lesser, hits, 1.0), convolve_kind(green_greater, mirrored, -1.0))
 
 
 def on_device(g_lesser, g_greater, coulomb, coupling, lag_slots):
@@ -128,28 +122,17 @@
         lax.all_to_all(g_lesser, "eng", split_axis=3, concat_axis=0, tiled=True),
         lax.all_to_all(g_greater, "eng", split_axis=3, concat_axis=0, tiled=True),
     )
-    polar_lesser, polar_greater = correlate_pair(el_lesser, el_greater, lag_slots)
-    polar_lesser, polar_greater = (
-        lax.all_to_all(polar_lesser, "eng", split_axis=0, concat_axis=3, tiled=True),
-        lax.all_to_all(polar_greater, "eng", split_axis=0, concat_axis=3, tiled=True),
-    )
+    polar = correlate(el_lesser, el_greater)
+    polar = lax.all_to_all(polar, "eng", split_axis=0, concat_axis=3, tiled=True)
     row_ids = lax.axis_index("blk") * row_count + jnp.arange(row_count, dtype=jnp.int32)
     all_rows = row_count * lax.axis_size("blk")
     kept_links = (coupling * (row_ids < all_rows - 1).astype(jnp.int32)).astype(jnp.bfloat16)
     v_both = jnp.stack([coulomb[:, 0], coulomb[:, 1] * kept_links[:, None, None]], axis=1)
-    stacked = jnp.concatenate([polar_lesser, polar_greater, v_both[None]], axis=0)
-    padded = padded_2(stacked, (("blk", 1),), 1)
-    screened = screen(padded[: 2 * own_energies], padded[2 * own_energies])
-    w_lesser = screened[:own_energies]
-    w_greater = screened[own_energies:]
-    w_el_lesser, w_el_greater = (
-        lax.all_to_all(w_lesser, "eng", split_axis=3, concat_axis=0, tiled=True),
-        lax.all_to_all(w_greater, "eng", split_axis=3, concat_axis=0, tiled=True),
-    )
-    green_lesser, green_greater = (el_lesser, el_greater)
-    self_lesser, self_greater = convolve_pair(
-        green_lesser, green_greater, w_el_lesser, w_el_greater, lag_slots
-    )
+    pad_v = padded_2(v_both[None], (("blk", 1),), 1)[0]
+    pad_p = padded_2(polar, (("blk", 1),), 1)
+    screened = screen(pad_p, pad_v)
+    w_el = lax.all_to_all(screened, "eng", split_axis=3, concat_axis=0, tiled=True)
+    self_lesser, self_greater = convolve_pair(el_lesser, el_greater, w_el, lag_slots)
     sigma_lesser, sigma_greater = (
         lax.all_to_all(self_lesser, "eng", split_axis=0, concat_axis=3, tiled=True),
         lax.all_to_all(self_greater, "eng", split_axis=0, concat_axis=3, tiled=True),

time: 305 us -> 236 us (0.77)
  waiting for transfers between devices: 177 us -> 125 us
  local copies, waits for them, and re-layouts: 31.3 us -> 23.7 us
  matrix products: 46.6 us -> 41.6 us
  starting transfers between devices: 44.7 us -> 39.8 us
    all_to_all x4 -> x2, waiting for transfers between devices: 82.8 us -> 37.6 us  [the longest x1 19.2 us: on_device(): lax.all_to_all(screened, 'eng', split_axis=3, concat_axis=0, tiled=True)]
    ppermute x1 -> x2, waiting for transfers between devices: 24.6 us -> 0.01 us  [padded_2(): after = lax.ppermute(leading, axis, down)]
    all_to_all x1, waiting for transfers between devices: 12.9 us -> 23.2 us  [on_device(): lax.all_to_all(self_lesser, 'eng', split_axis=0, concat_axis=3, tiled=True)]
    all_to_all x4 -> x2, starting transfers between devices: 17.5 us -> 8.03 us  [the longest x1 4.47 us: on_device(): lax.all_to_all(polar, 'eng', split_axis=0, concat_axis=3, tiled=True)]
    ppermute x1 -> x2, starting transfers between devices: 3.02 us -> 8.39 us  [padded_2(): before = lax.ppermute(last, axis, up)]
    slice x2, local copies, waits for them, and re-layouts: 5.28 us -> 0.17 us  [convolve_pair(): mirrored = jnp.roll(hits[::-1], 1)]
    dot_general x12, matrix products: 22.5 us -> 17.6 us  [product(): jnp.einsum(einsum_form, left_side, right_side, preferred_element_type=jnp...]
    ppermute x1 -> x2, waiting for transfers between devices: 1.18 us -> 5.82 us  [padded_2(): before = lax.ppermute(last, axis, up)]
  transfers between devices with their start and end apart: 10 -> 10, of which waited for: 10 -> 7; matrix products, arithmetic and copies ran while one was open for 12% -> 14% of each run, Pallas kernels for 0% -> 0%
where the time goes in v1:
time: 236 us; the launch traced here: 234 us
  waiting for transfers between devices  125 us (53%)
  matrix products  41.6 us (18%)
  starting transfers between devices  39.8 us (17%)
  local copies, waits for them, and re-layouts  23.7 us (10%)
  other arithmetic  2.66 us (1%)
    dot_general x14, matrix products, matmul(): jnp.dot(lookup_table, values_in, precision=lax.Precision.HIGHEST, preferr...  24 us
    all_to_all x1, waiting for transfers between devices, on_device(): lax.all_to_all(self_lesser, 'eng', split_axis=0, concat_axis=3, tiled=True)  23.2 us
    all_to_all x1, waiting for transfers between devices, on_device(): lax.all_to_all(g_greater, 'eng', split_axis=3, concat_axis=0, tiled=True)  22.8 us
    all_to_all x1, waiting for transfers between devices, on_device(): lax.all_to_all(g_lesser, 'eng', split_axis=3, concat_axis=0, tiled=True)  19.5 us
    all_to_all x1, waiting for transfers between devices, on_device(): lax.all_to_all(screened, 'eng', split_axis=3, concat_axis=0, tiled=True)  19.2 us
    all_to_all x1, waiting for transfers between devices, on_device(): lax.all_to_all(polar, 'eng', split_axis=0, concat_axis=3, tiled=True)  18.5 us
    dot_general x12, matrix products, product(): jnp.einsum(einsum_form, left_side, right_side, preferred_element_type=jnp...  17.6 us
    all_to_all x1, waiting for transfers between devices, on_device(): lax.all_to_all(self_greater, 'eng', split_axis=0, concat_axis=3, tiled=True)  15.5 us
  transfers between devices with their start and end apart: 10, of which 7 were waited for; matrix products, arithmetic and copies ran while one was open for 14% of the time, Pallas kernels for 0%

profile of v1, /device:TPU:1, one launch (start us, length us, event | category | flops | bytes accessed | tf_op | source)
XLA Modules:
  0.0 234.0 jit_solution(335535677020048402)
XLA Ops:
  0.6 3.1 %copy.127 = bf16[4,1,2,256,256]{4,0,2,1,3:T(4,128)(2,1)} copy(bf16[4,1,2,256,256]{4,3,2,1,0:T(8,128)(2,1)} %param.6) | data formatting | bytes 2097152 | tf_op args[1]
  3.7 6.4 %all-to-all-start.1 = ((bf16[4,1,2,256,256]{4,0,2,1,3:T(4,128)(2,1)}), bf16[4,1,2,256,256]{4,0,2,1,3:T(4,128)(2,1)S(1)}, u32[]{:S(2)}, u32[]{:S(2)}) async-start(bf16[4,1,2,256,256]{4,0,2,1,3:T(4,128)(2,1)} %copy.127), calls=%async_computation.1 | async-start | bytes 2097152 | tf_op jit(solution)/shard_map/all_to_all | solution.py:123
  10.1 1.8 copy.125
  11.9 22.8 %all-to-all-done.1 = bf16[4,1,2,256,256]{4,0,2,1,3:T(4,128)(2,1)S(1)} async-done(((bf16[4,1,2,256,256]{4,0,2,1,3:T(4,128)(2,1)}), bf16[4,1,2,256,256]{4,0,2,1,3:T(4,128)(2,1)S(1)}, u32[]{:S(2)}, u32[]{:S(2)}) %all-to-all-start.1) | async-done | bytes 1048608 | tf_op jit(solution)/shard_map/all_to_all | solution.py:123
  34.7 4.9 %all-to-all-start = ((bf16[4,1,2,256,256]{4,0,2,1,3:T(4,128)(2,1)}), bf16[4,1,2,256,256]{4,0,2,1,3:T(4,128)(2,1)S(1)}, u32[]{:S(2)}, u32[]{:S(2)}) async-start(bf16[4,1,2,256,256]{4,0,2,1,3:T(4,128)(2,1)} %copy.125), calls=%async_computation | async-start | bytes 2097152 | tf_op jit(solution)/shard_map/all_to_all | solution.py:122
  40.5 2.4 %fusion.74 = f32[32,16384]{1,0:T(8,128)} fusion(bf16[32,16384]{1,0:T(8,128)(2,1)S(1)} %reshape.187), kind=kOutput, calls=%fused_computation.104 | convolution fusion | flops 201340928 | bytes 3145728 | tf_op jit(solution)/shard_map/dot_general | solution.py:73
  42.8 2.4 %fusion.84 = f32[32,16384]{1,0:T(8,128)} fusion(bf16[32,16384]{1,0:T(8,128)(2,1)S(1)} %reshape.187), kind=kOutput, calls=%fused_computation.106 | convolution fusion | flops 201340928 | bytes 3145728 | tf_op jit(solution)/shard_map/dot_general | solution.py:73
  45.2 19.5 %all-to-all-done = bf16[4,1,2,256,256]{4,0,2,1,3:T(4,128)(2,1)S(1)} async-done(((bf16[4,1,2,256,256]{4,0,2,1,3:T(4,128)(2,1)}), bf16[4,1,2,256,256]{4,0,2,1,3:T(4,128)(2,1)S(1)}, u32[]{:S(2)}, u32[]{:S(2)}) %all-to-all-start) | async-done | bytes 1048608 | tf_op jit(solution)/shard_map/all_to_all | solution.py:122
  68.4 2.1 fusion.23
  70.5 2.3 fusion.3
  74.0 4.5 %all-to-all-start.2 = ((bf16[32,1,2,32,256]{4,3,2,1,0:T(8,128)(2,1)}), bf16[32,1,2,32,256]{4,3,2,1,0:T(8,128)(2,1)S(1)}, u32[]{:S(2)}, u32[]{:S(2)}) async-start(bf16[32,1,2,32,256]{4,3,2,1,0:T(8,128)(2,1)} %bitcast.181), calls=%async_computation.2 | async-start | bytes 2097152 | tf_op jit(solution)/shard_map/all_to_all | solution.py:126
  79.2 3.8 %collective-permute-start = (bf16[1,1,2,256,256]{4,3,2,1,0:T(8,128)(2,1)S(1)}, bf16[1,1,2,256,256]{4,3,2,1,0:T(8,128)(2,1)}, u32[]{:S(2)}, u32[]{:S(2)}) collective-permute-start(bf16[1,1,2,256,256]{4,3,2,1,0:T(8,128)(2,1)S(1)} %maximum_bitcast_fusion.1), channel_id=1, source_target_pairs={{0,8},{8,16},{16,24},{1,9},{9,17},{17,25},{2,10},{10,18},{18,26},{... | collective-permute-start | bytes 786440 | tf_op jit(solution)/shard_map/ppermute | solution.py:16
  83.0 2.1 collective-permute-start.1
  85.1 18.5 %all-to-all-done.2 = bf16[32,1,2,32,256]{4,3,2,1,0:T(8,128)(2,1)S(1)} async-done(((bf16[32,1,2,32,256]{4,3,2,1,0:T(8,128)(2,1)}), bf16[32,1,2,32,256]{4,3,2,1,0:T(8,128)(2,1)S(1)}, u32[]{:S(2)}, u32[]{:S(2)}) %all-to-all-start.2) | async-done | bytes 1048608 | tf_op jit(solution)/shard_map/all_to_all | solution.py:126
  107.2 4.6 %collective-permute-start.2 = (bf16[4,1,2,256,256]{3,4,0,2,1:T(8,128)(2,1)}, bf16[4,1,2,256,256]{3,4,0,2,1:T(8,128)(2,1)S(1)}, u32[]{:S(2)}, u32[]{:S(2)}) collective-permute-start(bf16[4,1,2,256,256]{3,4,0,2,1:T(8,128)(2,1)} %copy.131), channel_id=1, source_target_pairs={{0,8},{8,16},{16,24},{1,9},{9,17},{17,25},{2,10},{10,18},{18,26},{... | collective-permute-start | bytes 3145736 | tf_op jit(solution)/shard_map/ppermute | solution.py:16
  112.9 1.9 collective-permute-start.3
  118.0 5.8 %collective-permute-done.2 = bf16[4,1,2,256,256]{3,4,0,2,1:T(8,128)(2,1)S(1)} collective-permute-done((bf16[4,1,2,256,256]{3,4,0,2,1:T(8,128)(2,1)}, bf16[4,1,2,256,256]{3,4,0,2,1:T(8,128)(2,1)S(1)}, u32[]{:S(2)}, u32[]{:S(2)}) %collective-permute-start.2) | collective-permute-done | bytes 1048608 | tf_op jit(solution)/shard_map/ppermute | solution.py:16
  126.8 3.2 %fusion.43 = f32[256,4,256]{2,0,1:T(8,128)} fusion(f32[4,256,256]{2,1,0:T(8,128)} %fusion.47, bf16[4,1,2,256,256]{3,4,0,2,1:T(8,128)(2,1)} %copy-done.11, bf16[3,2,256,256]{3,2,1,0:T(8,128)(2,1)} %copy-done.6), kind=kOutput, calls=%fused_computation.55 | convolution fusion | flops 268959744 | bytes 2883584 | tf_op jit(solution)/shard_map/krab,rbc->krac/dot_general | solution.py:23
  130.0 1.6 convolution_add_fusion.4
  135.5 2.8 %fusion.39 = bf16[4,1,1,256,256]{3,4,0,2,1:T(8,128)(2,1)} fusion(f32[256,4,256]{2,0,1:T(8,128)} %convolution_add_fusion.1, bf16[4,1,2,256,256]{3,4,0,2,1:T(8,128)(2,1)} %collective-permute-done.3, bf16[3,2,256,256]{3,2,1,0:T(8,128)(2,1)S(1)} %copy-done.7), kind=kOutput, calls=%fused_computation.51 | convolution fusion | flops 269221888 | bytes 2359296 | tf_op jit(solution)/shard_map/krab,rcb->krac/dot_general | solution.py:23
  139.6 1.8 copy.147
  141.4 3.6 %all-to-all-start.3 = ((bf16[4,1,2,256,256]{4,0,2,1,3:T(4,128)(2,1)}), bf16[4,1,2,256,256]{4,0,2,1,3:T(4,128)(2,1)S(1)}, u32[]{:S(2)}, u32[]{:S(2)}) async-start(bf16[4,1,2,256,256]{4,0,2,1,3:T(4,128)(2,1)} %copy.147), calls=%async_computation.3 | async-start | bytes 2097152 | tf_op jit(solution)/shard_map/all_to_all | solution.py:134
  145.4 19.2 %all-to-all-done.3 = bf16[4,1,2,256,256]{4,0,2,1,3:T(4,128)(2,1)S(1)} async-done(((bf16[4,1,2,256,256]{4,0,2,1,3:T(4,128)(2,1)}), bf16[4,1,2,256,256]{4,0,2,1,3:T(4,128)(2,1)S(1)}, u32[]{:S(2)}, u32[]{:S(2)}) %all-to-all-start.3) | async-done | bytes 1048608 | tf_op jit(solution)/shard_map/all_to_all | solution.py:134
  170.2 2.0 fusion.9
  172.2 2.2 fusion.5
  175.6 4.5 %all-to-all-start.5 = ((bf16[32,1,2,32,256]{4,3,2,1,0:T(8,128)(2,1)}), bf16[32,1,2,32,256]{4,3,2,1,0:T(8,128)(2,1)}, u32[]{:S(2)}, u32[]{:S(2)}) async-start(bf16[32,1,2,32,256]{4,3,2,1,0:T(8,128)(2,1)} %bitcast.182), calls=%async_computation.5 | async-start | bytes 2097152 | tf_op jit(solution)/shard_map/all_to_all | solution.py:138
  182.7 2.1 fusion.16
  184.9 2.3 fusion.4
  188.4 15.5 %all-to-all-done.5 = bf16[32,1,2,32,256]{4,3,2,1,0:T(8,128)(2,1)} async-done(((bf16[32,1,2,32,256]{4,3,2,1,0:T(8,128)(2,1)}), bf16[32,1,2,32,256]{4,3,2,1,0:T(8,128)(2,1)}, u32[]{:S(2)}, u32[]{:S(2)}) %all-to-all-start.5) | async-done | bytes 1048608 | tf_op jit(solution)/shard_map/all_to_all | solution.py:138
  203.9 3.6 %all-to-all-start.4 = ((bf16[32,1,2,32,256]{4,3,2,1,0:T(8,128)(2,1)}), bf16[32,1,2,32,256]{4,3,2,1,0:T(8,128)(2,1)S(1)}, u32[]{:S(2)}, u32[]{:S(2)}) async-start(bf16[32,1,2,32,256]{4,3,2,1,0:T(8,128)(2,1)} %bitcast.58), calls=%async_computation.4 | async-start | bytes 2097152 | tf_op jit(solution)/shard_map/all_to_all | solution.py:137
  207.5 2.3 copy.153
  209.8 23.2 %all-to-all-done.4 = bf16[32,1,2,32,256]{4,3,2,1,0:T(8,128)(2,1)S(1)} async-done(((bf16[32,1,2,32,256]{4,3,2,1,0:T(8,128)(2,1)}), bf16[32,1,2,32,256]{4,3,2,1,0:T(8,128)(2,1)S(1)}, u32[]{:S(2)}, u32[]{:S(2)}) %all-to-all-start.4) | async-done | bytes 1048608 | tf_op jit(solution)/shard_map/all_to_all | solution.py:137
  (69 shorter events, 33.6 us)
Async XLA Ops:
  0.6 9.5 %copy-start.12 = (bf16[4,1,2,256,256]{4,3,2,1,0:T(8,128)(2,1)S(1)}, bf16[4,1,2,256,256]{4,3,2,1,0:T(8,128)(2,1)}, u32[]{:S(2)}) copy-start(bf16[4,1,2,256,256]{4,3,2,1,0:T(8,128)(2,1)} %param.5) | copy-start | bytes 3145732
  3.7 31.0 %all-to-all-start.1 = ((bf16[4,1,2,256,256]{4,0,2,1,3:T(4,128)(2,1)}), bf16[4,1,2,256,256]{4,0,2,1,3:T(4,128)(2,1)S(1)}, u32[]{:S(2)}, u32[]{:S(2)}) async-start(bf16[4,1,2,256,256]{4,0,2,1,3:T(4,128)(2,1)} %copy.127), calls=%async_computation.1 | async-start | bytes 2097152 | tf_op jit(solution)/shard_map/all_to_all | solution.py:123
  34.7 30.0 %all-to-all-start = ((bf16[4,1,2,256,256]{4,0,2,1,3:T(4,128)(2,1)}), bf16[4,1,2,256,256]{4,0,2,1,3:T(4,128)(2,1)S(1)}, u32[]{:S(2)}, u32[]{:S(2)}) async-start(bf16[4,1,2,256,256]{4,0,2,1,3:T(4,128)(2,1)} %copy.125), calls=%async_computation | async-start | bytes 2097152 | tf_op jit(solution)/shard_map/all_to_all | solution.py:122
  65.6 2.1 copy-start.4
  66.6 1.7 copy-start.2
  68.4 2.1 copy-start
  72.8 6.4 %copy-start.13 = (bf16[1,2,256,256]{3,2,1,0:T(8,128)(2,1)S(1)}, bf16[1,2,256,256]{3,2,1,0:T(8,128)(2,1)}, u32[]{:S(2)}) copy-start(bf16[1,2,256,256]{3,2,1,0:T(8,128)(2,1)} %param.7) | copy-start | bytes 786436
  74.0 29.6 %all-to-all-start.2 = ((bf16[32,1,2,32,256]{4,3,2,1,0:T(8,128)(2,1)}), bf16[32,1,2,32,256]{4,3,2,1,0:T(8,128)(2,1)S(1)}, u32[]{:S(2)}, u32[]{:S(2)}) async-start(bf16[32,1,2,32,256]{4,3,2,1,0:T(8,128)(2,1)} %bitcast.181), calls=%async_computation.2 | async-start | bytes 2097152 | tf_op jit(solution)/shard_map/all_to_all | solution.py:126
  79.2 32.6 %collective-permute-start = (bf16[1,1,2,256,256]{4,3,2,1,0:T(8,128)(2,1)S(1)}, bf16[1,1,2,256,256]{4,3,2,1,0:T(8,128)(2,1)}, u32[]{:S(2)}, u32[]{:S(2)}) collective-permute-start(bf16[1,1,2,256,256]{4,3,2,1,0:T(8,128)(2,1)S(1)} %maximum_bitcast_fusion.1), channel_id=1, source_target_pairs={{0,8},{8,16},{16,24},{1,9},{9,17},{17,25},{2,10},{10,18},{18,26},{... | collective-permute-start | bytes 786440 | tf_op jit(solution)/shard_map/ppermute | solution.py:16
  83.0 28.8 %collective-permute-start.1 = (bf16[1,1,2,256,256]{4,3,2,1,0:T(8,128)(2,1)S(1)}, bf16[1,1,2,256,256]{4,3,2,1,0:T(8,128)(2,1)}, u32[]{:S(2)}, u32[]{:S(2)}) collective-permute-start(bf16[1,1,2,256,256]{4,3,2,1,0:T(8,128)(2,1)S(1)} %maximum_bitcast_fusion.1), channel_id=1, source_target_pairs={{8,0},{16,8},{24,16},{9,1},{17,9},{25,17},{10,2},{18,10},{26,18},{... | collective-permute-start | bytes 786440 | tf_op jit(solution)/shard_map/ppermute | solution.py:17
  103.6 1.0 copy-start.8
  107.2 16.7 %collective-permute-start.2 = (bf16[4,1,2,256,256]{3,4,0,2,1:T(8,128)(2,1)}, bf16[4,1,2,256,256]{3,4,0,2,1:T(8,128)(2,1)S(1)}, u32[]{:S(2)}, u32[]{:S(2)}) collective-permute-start(bf16[4,1,2,256,256]{3,4,0,2,1:T(8,128)(2,1)} %copy.131), channel_id=1, source_target_pairs={{0,8},{8,16},{16,24},{1,9},{9,17},{17,25},{2,10},{10,18},{18,26},{... | collective-permute-start | bytes 3145736 | tf_op jit(solution)/shard_map/ppermute | solution.py:16
  112.9 12.5 %copy-start.6 = (bf16[3,2,256,256]{3,2,1,0:T(8,128)(2,1)}, bf16[3,2,256,256]{3,2,1,0:T(8,128)(2,1)S(1)}, u32[]{:S(2)}) copy-start(bf16[3,2,256,256]{3,2,1,0:T(8,128)(2,1)S(1)} %maximum_bitcast_fusion) | copy-start | bytes 2359300
  112.9 18.7 %collective-permute-start.3 = (bf16[4,1,2,256,256]{3,4,0,2,1:T(8,128)(2,1)}, bf16[4,1,2,256,256]{3,4,0,2,1:T(8,128)(2,1)}, u32[]{:S(2)}, u32[]{:S(2)}) collective-permute-start(bf16[4,1,2,256,256]{3,4,0,2,1:T(8,128)(2,1)} %copy.131), channel_id=1, source_target_pairs={{8,0},{16,8},{24,16},{9,1},{17,9},{25,17},{10,2},{18,10},{26,18},{... | collective-permute-start | bytes 3145736 | tf_op jit(solution)/shard_map/ppermute | solution.py:17
  123.8 1.6 copy-start.11
  126.8 3.2 %copy-start.7 = (bf16[3,2,256,256]{3,2,1,0:T(8,128)(2,1)S(1)}, bf16[3,2,256,256]{3,2,1,0:T(8,128)(2,1)}, u32[]{:S(2)}) copy-start(bf16[3,2,256,256]{3,2,1,0:T(8,128)(2,1)} %copy-done.6) | copy-start | bytes 2359300
  130.0 1.7 copy-start.9
  131.6 2.6 %copy-start.10 = (f32[256,4,256]{2,0,1:T(8,128)S(1)}, f32[256,4,256]{2,0,1:T(8,128)}, u32[]{:S(2)}) copy-start(f32[256,4,256]{2,0,1:T(8,128)} %fusion.50) | copy-start | bytes 3145732
  139.6 5.4 %copy-start.14 = (s32[32]{0:T(128)S(1)}, s32[32]{0:T(128)}, u32[]{:S(2)}) copy-start(s32[32]{0:T(128)} %param.9) | copy-start | bytes 388
  141.4 23.1 %all-to-all-start.3 = ((bf16[4,1,2,256,256]{4,0,2,1,3:T(4,128)(2,1)}), bf16[4,1,2,256,256]{4,0,2,1,3:T(4,128)(2,1)S(1)}, u32[]{:S(2)}, u32[]{:S(2)}) async-start(bf16[4,1,2,256,256]{4,0,2,1,3:T(4,128)(2,1)} %copy.147), calls=%async_computation.3 | async-start | bytes 2097152 | tf_op jit(solution)/shard_map/all_to_all | solution.py:134
  167.4 2.1 copy-start.5
  168.4 1.7 copy-start.3
  175.6 28.3 %all-to-all-start.5 = ((bf16[32,1,2,32,256]{4,3,2,1,0:T(8,128)(2,1)}), bf16[32,1,2,32,256]{4,3,2,1,0:T(8,128)(2,1)}, u32[]{:S(2)}, u32[]{:S(2)}) async-start(bf16[32,1,2,32,256]{4,3,2,1,0:T(8,128)(2,1)} %bitcast.182), calls=%async_computation.5 | async-start | bytes 2097152 | tf_op jit(solution)/shard_map/all_to_all | solution.py:138
  181.2 1.6 copy-start.1
  203.9 29.1 %all-to-all-start.4 = ((bf16[32,1,2,32,256]{4,3,2,1,0:T(8,128)(2,1)}), bf16[32,1,2,32,256]{4,3,2,1,0:T(8,128)(2,1)S(1)}, u32[]{:S(2)}, u32[]{:S(2)}) async-start(bf16[32,1,2,32,256]{4,3,2,1,0:T(8,128)(2,1)} %bitcast.58), calls=%async_computation.4 | async-start | bytes 2097152 | tf_op jit(solution)/shard_map/all_to_all | solution.py:137

commit v2 on v1

v2 whole, which is shorter than its diff:
```python
import functools

import jax
import jax.numpy as jnp
from jax import lax
from jax.experimental import pallas as pl
from jax.experimental.pallas import tpu as pltpu
from jax.sharding import PartitionSpec as P

MESH = pl.DeviceIdType.MESH
LANES = 128
PACK = 16
DIRECT = 8


def correlate(first, second, sign=1.0):
    count = first.shape[0]
    if sign > 0 and count > DIRECT and count % 2 == 0:
        half = count // 2
        first_lo, first_hi = first[:half], first[half:]
        second_lo, second_hi = second[:half] * 0.5, second[half:] * 0.5
        even = correlate(first_lo + first_hi, second_lo + second_hi)
        odd = correlate(first_lo - first_hi, second_lo - second_hi, -1.0)
        return jnp.concatenate([even + odd, even - odd], axis=0)
    wrapped = jnp.concatenate([first, first if sign > 0 else -first], axis=0)
    total = second[0:1] * wrapped[:count]
    for j in range(1, count):
        total = total + second[j : j + 1] * wrapped[j : j + count]
    return total


def convolve(first, second, sign=1.0):
    count = first.shape[0]
    if sign > 0 and count > DIRECT and count % 2 == 0:
        half = count // 2
        first_lo, first_hi = first[:half], first[half:]
        second_lo, second_hi = second[:half] * 0.5, second[half:] * 0.5
        even = convolve(first_lo + first_hi, second_lo + second_hi)
        odd = convolve(first_lo - first_hi, second_lo - second_hi, -1.0)
        return jnp.concatenate([even + odd, even - odd], axis=0)
    wrapped = jnp.concatenate([first if sign > 0 else -first, first], axis=0)
    total = second[0:1] * wrapped[count:]
    for j in range(1, count):
        total = total + second[j : j + 1] * wrapped[count - j : 2 * count - j]
    return total


def dot(left, right):
    return jnp.dot(left, right, preferred_element_type=jnp.float32)


def dot_t(left, right):
    return lax.dot_general(
        left, right, (((1,), (1,)), ((), ())), preferred_element_type=jnp.float32
    )


def kernel(
    n_blk,
    n_eng,
    gl_ref,
    gg_ref,
    v_ref,
    weight_ref,
    sl_ref,
    sg_ref,
    green,
    polar_el,
    polar,
    v_all,
    w_own,
    w_el,
    sigma,
    g_send,
    g_recv,
    p_send,
    p_recv,
    halo_send,
    halo_recv,
    v_send,
    v_recv,
    w_send,
    w_recv,
    s_send,
    s_recv,
    local_g,
    local_p,
    local_w,
    local_s,
    local_v,
):
    blk = lax.axis_index("blk")
    me = lax.axis_index("eng")
    own, blocks, size = gl_ref.shape[0], gl_ref.shape[2], gl_ref.shape[3]
    energies = own * n_eng
    rows = size // n_eng
    scale = energies ** (-0.5)
    has_left, has_right = blk > 0, blk < n_blk - 1
    g_refs, s_refs = (gl_ref, gg_ref), (sl_ref, sg_ref)

    def peer_of(step):
        return lax.rem(me + step, n_eng)

    def part(index, length):
        return pl.ds(pl.multiple_of(index * length, length), length)

    def remote(src, dst, send, recv, blk_to, eng_to):
        return pltpu.make_async_remote_copy(
            src_ref=src,
            dst_ref=dst,
            send_sem=send,
            recv_sem=recv,
            device_id=(blk_to, eng_to),
            device_id_type=MESH,
        )

    def each(body, low=1, high=n_eng):
        def run(step, carry):
            body(step)
            return carry

        lax.fori_loop(low, high, run, 0)

    def g_copy(kind, b, step):
        return remote(
            g_refs[kind].at[:, 0, b, part(peer_of(step), rows), :],
            green.at[kind, part(me, own), b],
            g_send.at[kind, b, step],
            g_recv.at[kind, b, step],
            blk,
            peer_of(step),
        )

    def g_local(kind, b):
        return pltpu.make_async_copy(
            g_refs[kind].at[:, 0, b, part(me, rows), :],
            green.at[kind, part(me, own), b],
            local_g.at[kind, b],
        )

    def p_copy(slot, b, step):
        return remote(
            polar_el.at[peer_of(step) * own + slot, b],
            polar.at[1, slot, b, part(me, rows), :],
            p_send.at[slot, b, step],
            p_recv.at[slot, b, step],
            blk,
            peer_of(step),
        )

    def p_local(slot, b):
        return pltpu.make_async_copy(
            polar_el.at[me * own + slot, b],
            polar.at[1, slot, b, part(me, rows), :],
            local_p.at[slot, b],
        )

    def halo_copy(slot, side):
        return remote(
            polar.at[1, slot],
            polar.at[2 - 2 * side, slot],
            halo_send.at[slot, side],
            halo_recv.at[slot, side],
            lax.rem(blk - 1 + 2 * side + n_blk, n_blk),
            me,
        )

    def v_copy(side):
        return remote(
            v_ref,
            v_all.at[2 - 2 * side],
            v_send.at[side],
            v_recv.at[side],
            lax.rem(blk - 1 + 2 * side + n_blk, n_blk),
            me,
        )

    def w_copy(slot, step):
        return remote(
            w_own.at[slot, :, part(peer_of(step), rows), :],
            w_el.at[me * own + slot],
            w_send.at[slot, step],
            w_recv.at[slot, step],
            blk,
            peer_of(step),
        )

    def w_local(slot):
        return pltpu.make_async_copy(
            w_own.at[slot, :, part(me, rows), :], w_el.at[me * own + slot], local_w.at[slot]
        )

    def s_copy(kind, b, step):
        return remote(
            sigma.at[kind, part(peer_of(step), own), b],
            s_refs[kind].at[:, 0, b, part(me, rows), :],
            s_send.at[kind, b, step],
            s_recv.at[kind, b, step],
            blk,
            peer_of(step),
        )

    def s_local(kind, b):
        return pltpu.make_async_copy(
            sigma.at[kind, part(me, own), b],
            s_refs[kind].at[:, 0, b, part(me, rows), :],
            local_s.at[kind, b],
        )

    barrier = pltpu.get_barrier_semaphore()

    def greet(step):
        pl.semaphore_signal(barrier, inc=1, device_id=(blk, peer_of(step)), device_id_type=MESH)

    each(greet)

    @pl.when(has_left)
    def _():
        pl.semaphore_signal(barrier, inc=1, device_id=(blk - 1, me), device_id_type=MESH)

    @pl.when(has_right)
    def _():
        pl.semaphore_signal(barrier, inc=1, device_id=(blk + 1, me), device_id_type=MESH)

    for b in range(blocks):
        for kind in range(2):
            g_local(kind, b).start()
    v_mine = pltpu.make_async_copy(v_ref, v_all.at[1], local_v.at[0])
    v_mine.start()

    pl.semaphore_wait(barrier, n_eng - 1 + has_left.astype(jnp.int32) + has_right.astype(jnp.int32))

    for b in range(blocks):
        for kind in range(2):
            each(lambda step: g_copy(kind, b, step).start())

    @pl.when(has_left)
    def _():
        v_copy(0).start()

    @pl.when(has_right)
    def _():
        v_copy(1).start()

    @pl.when(jnp.logical_not(has_left))
    def _():
        polar[0] = jnp.zeros(polar.shape[1:], polar.dtype)
        v_all[0] = jnp.zeros(v_all.shape[1:], v_all.dtype)

    @pl.when(jnp.logical_not(has_right))
    def _():
        polar[2] = jnp.zeros(polar.shape[1:], polar.dtype)
        v_all[2] = jnp.zeros(v_all.shape[1:], v_all.dtype)

    lane_tiles = size // LANES
    tiles = (rows // PACK) * lane_tiles
    half = PACK // 2

    def tile_of(tile):
        row, lane = lax.div(tile, lane_tiles), lax.rem(tile, lane_tiles)
        return part(row, PACK), part(lane, LANES)

    for b in range(blocks):
        for kind in range(2):
            g_local(kind, b).wait()
            each(lambda step: g_copy(kind, b, step).wait_recv())

        def polar_tile(tile):
            at = tile_of(tile)
            lesser = green[0, :, b, at[0], at[1]]
            greater = green[1, :, b, at[0], at[1]]
            out = []
            for top in (0, half):
                first = lesser.astype(jnp.float32)[:, top : top + half]
                second = greater.astype(jnp.float32)[:, top : top + half] * scale
                out.append(correlate(first, second))
            polar_el[:, b, at[0], at[1]] = jnp.concatenate(out, axis=1).astype(jnp.bfloat16)

        each(polar_tile, 0, tiles)

        def send_slot(slot):
            each(lambda step: p_copy(slot, b, step).start())
            p_local(slot, b).start()

        each(send_slot, 0, own)

    v_mine.wait()

    @pl.when(has_left)
    def _():
        v_copy(0).wait_send()
        v_copy(1).wait_recv()

    @pl.when(has_right)
    def _():
        v_copy(1).wait_send()
        v_copy(0).wait_recv()

    def screen_slot(slot):
        diag_minus, up_minus = polar[0, slot, 0], polar[0, slot, 1]
        diag_zero, up_zero = polar[1, slot, 0], polar[1, slot, 1]
        diag_plus, up_plus = polar[2, slot, 0], polar[2, slot, 1]
        q_minus = dot(v_all[0, 2], diag_minus) + dot_t(v_all[1, 0], up_minus)
        q_zero = (
            dot(v_all[0, 2], up_minus)
            + dot(v_all[1, 0], diag_zero)
            + dot_t(v_all[1, 1], up_zero)
        )
        q_plus = dot(v_all[1, 0], up_zero) + dot(v_all[1, 1], diag_plus)
        q_far = dot(v_all[1, 1], up_plus).astype(jnp.bfloat16)
        q_minus = q_minus.astype(jnp.bfloat16)
        q_zero = q_zero.astype(jnp.bfloat16)
        q_plus = q_plus.astype(jnp.bfloat16)
        w_diag = dot(q_minus, v_all[0, 1]) + dot(q_zero, v_all[1, 0]) + dot(q_plus, v_all[1, 2])
        w_upper = dot(q_zero, v_all[1, 1]) + dot(q_plus, v_all[2, 0]) + dot(q_far, v_all[2, 2])
        w_own[slot, 0] = w_diag.astype(jnp.bfloat16)
        w_own[slot, 1] = w_upper.astype(jnp.bfloat16)

    def screen_step(step):
        @pl.when(step < own)
        def _():
            for b in range(blocks):
                p_local(step, b).wait()
                each(lambda other: p_copy(step, b, other).wait_recv())

            @pl.when(has_left)
            def _():
                halo_copy(step, 0).start()

            @pl.when(has_right)
            def _():
                halo_copy(step, 1).start()

        @pl.when(step > 0)
        def _():
            slot = step - 1

            @pl.when(has_left)
            def _():
                halo_copy(slot, 1).wait_recv()

            @pl.when(has_right)
            def _():
                halo_copy(slot, 0).wait_recv()

            screen_slot(slot)
            each(lambda other: w_copy(slot, other).start())
            w_local(slot).start()

    each(screen_step, 0, own + 1)

    def take_slot(slot):
        w_local(slot).wait()
        each(lambda other: w_copy(slot, other).wait_recv())

    each(take_slot, 0, own)

    for b in range(blocks):

        def sigma_tile(tile):
            at = tile_of(tile)
            screened = w_el[:, b, at[0], at[1]]
            for kind, combine in ((0, convolve), (1, correlate)):
                values = green[kind, :, b, at[0], at[1]]
                out = []
                for top in (0, half):
                    first = values.astype(jnp.float32)[:, top : top + half]
                    second = screened.astype(jnp.float32)[:, top : top + half] * weight_ref[kind]
                    out.append(combine(first, second))
                sigma[kind, :, b, at[0], at[1]] = jnp.concatenate(out, axis=1).astype(jnp.bfloat16)

        each(sigma_tile, 0, tiles)
        for kind in range(2):
            each(lambda step: s_copy(kind, b, step).start())
            s_local(kind, b).start()

    for b in range(blocks):
        for kind in range(2):
            each(lambda step: g_copy(kind, b, step).wait_send())

        def sent_slot(slot):
            each(lambda step: p_copy(slot, b, step).wait_send())

        each(sent_slot, 0, own)

    def sent_rest(slot):
        each(lambda step: w_copy(slot, step).wait_send())

        @pl.when(has_left)
        def _():
            halo_copy(slot, 0).wait_send()

        @pl.when(has_right)
        def _():
            halo_copy(slot, 1).wait_send()

    each(sent_rest, 0, own)
    for b in range(blocks):
        for kind in range(2):
            s_local(kind, b).wait()
            each(lambda step: s_copy(kind, b, step).wait())


def on_device(n_blk, n_eng, g_lesser, g_greater, coulomb, coupling, lag_slots):
    own, row_count, blocks, size = g_lesser.shape[:4]
    energies = own * n_eng
    rows = size // n_eng
    row_ids = lax.axis_index("blk") * row_count + jnp.arange(row_count, dtype=jnp.int32)
    kept_links = (coupling * (row_ids < row_count * n_blk - 1).astype(jnp.int32)).astype(jnp.bfloat16)
    upper = coulomb[0, 1] * kept_links[0]
    v_both = jnp.stack([coulomb[0, 0], upper, upper.T])
    slot_ids = jnp.arange(energies, dtype=jnp.int32)
    hits = jnp.sum((lag_slots[:, None] == slot_ids[None, :]).astype(jnp.float32), axis=0)
    mirrored = jnp.sum(
        (lag_slots[:, None] == ((energies - slot_ids) % energies)[None, :]).astype(jnp.float32), axis=0
    )
    weights = jnp.stack([hits, mirrored]) * energies ** (-0.5)
    weights = jnp.broadcast_to(weights[:, :, None, None], (2, energies, PACK // 2, LANES))
    dma, bf16 = pltpu.SemaphoreType.DMA, jnp.bfloat16
    element = (energies, blocks, rows, size)
    any_space = pl.BlockSpec(memory_space=pl.ANY)
    vmem = pl.BlockSpec(memory_space=pltpu.VMEM)
    out = jax.ShapeDtypeStruct(g_lesser.shape, bf16)
    return pl.pallas_call(
        functools.partial(kernel, n_blk, n_eng),
        out_shape=(out, out),
        in_specs=[any_space, any_space, vmem, vmem],
        out_specs=(any_space, any_space),
        scratch_shapes=[
            pltpu.VMEM((2, *element), bf16),
            pltpu.VMEM(element, bf16),
            pltpu.VMEM((3, own, blocks, size, size), bf16),
            pltpu.VMEM((3, 3, size, size), bf16),
            pltpu.VMEM((own, blocks, size, size), bf16),
            pltpu.VMEM(element, bf16),
            pltpu.VMEM((2, *element), bf16),
            dma((2, blocks, n_eng)),
            dma((2, blocks, n_eng)),
            dma((own, blocks, n_eng)),
            dma((own, blocks, n_eng)),
            dma((own, 2)),
            dma((own, 2)),
            dma((2,)),
            dma((2,)),
            dma((own, n_eng)),
            dma((own, n_eng)),
            dma((2, blocks, n_eng)),
            dma((2, blocks, n_eng)),
            dma((2, blocks)),
            dma((own, blocks)),
            dma((own,)),
            dma((2, blocks)),
            dma((1,)),
        ],
        compiler_params=pltpu.CompilerParams(
            collective_id=0, has_side_effects=True, vmem_limit_bytes=40 * 1024 * 1024
        ),
    )(g_lesser, g_greater, v_both, weights)


def solution(mesh):
    n_blk, n_eng = mesh.shape["blk"], mesh.shape["eng"]
    return jax.shard_map(
        functools.partial(on_device, n_blk, n_eng),
        mesh=mesh,
        in_specs=(
            P("eng", "blk", None, None, None),
            P("eng", "blk", None, None, None),
            P("blk", None, None, None),
            P("blk"),
            P(),
        ),
        out_specs=(P("eng", "blk", None, None, None), P("eng", "blk", None, None, None)),
        check_vma=False,
    )
```

time: 236 us -> 153 us (0.65)
  Pallas kernels: 0 us -> 146 us
  waiting for transfers between devices: 125 us -> 0 us
  matrix products: 41.6 us -> 0 us
  starting transfers between devices: 39.8 us -> 0 us
  local copies, waits for them, and re-layouts: 23.7 us -> 3.49 us
    pallas_call x0 -> x1, Pallas kernels: none -> 146 us  [on_device(): pl.pallas_call(functools.partial(kernel, n_blk, n_eng), out_shape=(out, o...]
    all_to_all x6 -> x0, waiting for transfers between devices: 119 us -> none  [the longest x1 23.2 us: on_device(): lax.all_to_all(self_lesser, 'eng', split_axis=0, concat_axis=3, tiled=True)]
    dot_general x26 -> x0, matrix products: 41.6 us -> none  [the longest x14 24 us: matmul(): jnp.dot(lookup_table, values_in, precision=lax.Precision.HIGHEST, preferr...]
    all_to_all x6 -> x0, starting transfers between devices: 27.4 us -> none  [the longest x1 6.38 us: on_device(): lax.all_to_all(g_greater, 'eng', split_axis=3, concat_axis=0, tiled=True)]
    ppermute x4 -> x0, starting transfers between devices: 12.4 us -> none  [the longest x2 8.39 us: padded_2(): before = lax.ppermute(last, axis, up)]
    unnamed x35 -> x9, local copies, waits for them, and re-layouts: 11.4 us -> 3.25 us
    all_to_all x8 -> x0, local copies, waits for them, and re-layouts: 7.73 us -> none  [the longest x2 2.61 us: on_device(): lax.all_to_all(polar, 'eng', split_axis=0, concat_axis=3, tiled=True)]
    ppermute x4 -> x0, waiting for transfers between devices: 5.83 us -> none  [the longest x2 5.82 us: padded_2(): before = lax.ppermute(last, axis, up)]
  transfers between devices with their start and end apart: 10 -> 0, of which waited for: 7 -> 0; matrix products, arithmetic and copies ran while one was open for 14% -> 0% of each run, Pallas kernels for 0% -> 0%
where the time goes in v2:
time: 153 us; the launch traced here: 152 us
  Pallas kernels  146 us (95%)
  local copies, waits for them, and re-layouts  3.49 us (2%)
    pallas_call x1, Pallas kernels, on_device(): pl.pallas_call(functools.partial(kernel, n_blk, n_eng), out_shape=(out, o...  146 us
    unnamed x9, local copies, waits for them, and re-layouts  3.25 us

profile of v2, /device:TPU:1, one launch (start us, length us, event | category | flops | bytes accessed | tf_op | source)
XLA Modules:
  0.0 152.2 jit_solution(16545402045467983923)
XLA Ops:
  0.6 0.0 copy-start.2
  1.4 0.7 convert_reduce_fusion.1
  2.1 0.1 broadcast_in_dim.2.weight_ref
  2.2 0.0 copy-done.2
  2.3 0.0 copy-start
  2.3 0.0 copy-start.1
  2.3 0.1 copy.11
  2.4 0.1 copy.10
  2.6 0.9 copy-done
  3.5 0.3 copy-done.1
  3.8 146.5 %shard_map.68 = (bf16[4,1,2,256,256]{4,3,2,1,0:T(8,128)(2,1)S(1)}, bf16[4,1,2,256,256]{4,3,2,1,0:T(8,128)(2,1)S(1)}) custom-call(bf16[4,1,2,256,256]{4,3,2,1,0:T(8,128)(2,1)S(1)} %copy-done, bf16[4,1,2,256,256]{4,3,2,1,0:T(8,128)(2,1)S(1)} %copy-done.1, bf16[3,256,256]{2,1,0:T(8,128)(2,1)S(1)} %pad_maximum_fusion.v_ref, ...), custom_call_target="tpu_custom_call" | custom-call | tf_op jit(solution)/shard_map/pallas_call | solution.py:424
  150.3 1.0 copy.15
  151.3 1.0 copy.16
  (5 shorter events, 0.1 us)
Async XLA Ops:
  0.6 1.6 %copy-start.2 = (bf16[1,2,256,256]{3,2,1,0:T(8,128)(2,1)S(1)}, bf16[1,2,256,256]{3,2,1,0:T(8,128)(2,1)}, u32[]{:S(2)}) copy-start(bf16[1,2,256,256]{3,2,1,0:T(8,128)(2,1)} %param.7) | copy-start | bytes 786436
  2.3 1.2 copy-start
  2.3 1.5 %copy-start.1 = (bf16[4,1,2,256,256]{4,3,2,1,0:T(8,128)(2,1)S(1)}, bf16[4,1,2,256,256]{4,3,2,1,0:T(8,128)(2,1)}, u32[]{:S(2)}) copy-start(bf16[4,1,2,256,256]{4,3,2,1,0:T(8,128)(2,1)} %gg_ref.1) | copy-start | bytes 3145732

commit v3 on v2

--- a/solution.py
+++ b/solution.py
@@ -155,12 +155,12 @@
             local_p.at[slot, b],
         )
 
-    def halo_copy(slot, side):
-        return remote(
-            polar.at[1, slot],
-            polar.at[2 - 2 * side, slot],
-            halo_send.at[slot, side],
-            halo_recv.at[slot, side],
+    def halo_copy(slot, side, b):
+        return remote(
+            polar.at[1, slot, b],
+            polar.at[2 - 2 * side, slot, b],
+            halo_send.at[slot, side, b],
+            halo_recv.at[slot, side, b],
             lax.rem(blk - 1 + 2 * side + n_blk, n_blk),
             me,
         )
@@ -316,32 +316,39 @@
         w_own[slot, 0] = w_diag.astype(jnp.bfloat16)
         w_own[slot, 1] = w_upper.astype(jnp.bfloat16)
 
+    def pass_on(slot, b):
+        p_local(slot, b).wait()
+        each(lambda other: p_copy(slot, b, other).wait_recv())
+
+        @pl.when(has_left)
+        def _():
+            halo_copy(slot, 0, b).start()
+
+        @pl.when(has_right)
+        def _():
+            halo_copy(slot, 1, b).start()
+
+    for b in range(blocks - 1):
+        each(lambda slot: pass_on(slot, b), 0, own)
+
     def screen_step(step):
         @pl.when(step < own)
         def _():
-            for b in range(blocks):
-                p_local(step, b).wait()
-                each(lambda other: p_copy(step, b, other).wait_recv())
+            pass_on(step, blocks - 1)
+
+        @pl.when(step > 0)
+        def _():
+            slot = step - 1
 
             @pl.when(has_left)
             def _():
-                halo_copy(step, 0).start()
+                for b in range(blocks):
+                    halo_copy(slot, 1, b).wait_recv()
 
             @pl.when(has_right)
             def _():
-                halo_copy(step, 1).start()
-
-        @pl.when(step > 0)
-        def _():
-            slot = step - 1
-
-            @pl.when(has_left)
-            def _():
-                halo_copy(slot, 1).wait_recv()
-
-            @pl.when(has_right)
-            def _():
-                halo_copy(slot, 0).wait_recv()
+                for b in range(blocks):
+                    halo_copy(slot, 0, b).wait_recv()
 
             screen_slot(slot)
             each(lambda other: w_copy(slot, other).start())
@@ -356,11 +363,11 @@
     each(take_slot, 0, own)
 
     for b in range(blocks):
-
-        def sigma_tile(tile):
-            at = tile_of(tile)
-            screened = w_el[:, b, at[0], at[1]]
-            for kind, combine in ((0, convolve), (1, correlate)):
+        for kind, combine in ((0, convolve), (1, correlate)):
+
+            def sigma_tile(tile):
+                at = tile_of(tile)
+                screened = w_el[:, b, at[0], at[1]]
                 values = green[kind, :, b, at[0], at[1]]
                 out = []
                 for top in (0, half):
@@ -369,8 +376,7 @@
                     out.append(combine(first, second))
                 sigma[kind, :, b, at[0], at[1]] = jnp.concatenate(out, axis=1).astype(jnp.bfloat16)
 
-        each(sigma_tile, 0, tiles)
-        for kind in range(2):
+            each(sigma_tile, 0, tiles)
             each(lambda step: s_copy(kind, b, step).start())
             s_local(kind, b).start()
 
@@ -388,11 +394,13 @@
 
         @pl.when(has_left)
         def _():
-            halo_copy(slot, 0).wait_send()
+            for b in range(blocks):
+                halo_copy(slot, 0, b).wait_send()
 
         @pl.when(has_right)
         def _():
-            halo_copy(slot, 1).wait_send()
+            for b in range(blocks):
+                halo_copy(slot, 1, b).wait_send()
 
     each(sent_rest, 0, own)
     for b in range(blocks):
@@ -438,8 +446,8 @@
             dma((2, blocks, n_eng)),
             dma((own, blocks, n_eng)),
             dma((own, blocks, n_eng)),
-            dma((own, 2)),
-            dma((own, 2)),
+            dma((own, 2, blocks)),
+            dma((own, 2, blocks)),
             dma((2,)),
             dma((2,)),
             dma((own, n_eng)),

time: 153 us -> 152 us (level)
  no operation moved by 1% of the time
where the time goes in v3:
time: 152 us; the launch traced here: 151 us
  Pallas kernels  145 us (95%)
  local copies, waits for them, and re-layouts  3.49 us (2%)
    pallas_call x1, Pallas kernels, on_device(): pl.pallas_call(functools.partial(kernel, n_blk, n_eng), out_shape=(out, o...  145 us
    unnamed x9, local copies, waits for them, and re-layouts  3.25 us

profile of v3, /device:TPU:1, one launch (start us, length us, event | category | flops | bytes accessed | tf_op | source)
XLA Modules:
  0.0 150.9 jit_solution(15700588370243593779)
XLA Ops:
  0.6 0.0 copy-start.2
  1.4 0.7 convert_reduce_fusion.1
  2.1 0.1 broadcast_in_dim.2.weight_ref
  2.2 0.0 copy-done.2
  2.3 0.0 copy-start
  2.3 0.0 copy-start.1
  2.3 0.1 copy.11
  2.4 0.1 copy.10
  2.6 0.9 copy-done
  3.5 0.3 copy-done.1
  3.8 145.2 %shard_map.68 = (bf16[4,1,2,256,256]{4,3,2,1,0:T(8,128)(2,1)S(1)}, bf16[4,1,2,256,256]{4,3,2,1,0:T(8,128)(2,1)S(1)}) custom-call(bf16[4,1,2,256,256]{4,3,2,1,0:T(8,128)(2,1)S(1)} %copy-done, bf16[4,1,2,256,256]{4,3,2,1,0:T(8,128)(2,1)S(1)} %copy-done.1, bf16[3,256,256]{2,1,0:T(8,128)(2,1)S(1)} %pad_maximum_fusion.v_ref, ...), custom_call_target="tpu_custom_call" | custom-call | tf_op jit(solution)/shard_map/pallas_call | solution.py:432
  149.0 1.0 copy.15
  150.0 1.0 copy.16
  (5 shorter events, 0.1 us)
Async XLA Ops:
  0.6 1.6 %copy-start.2 = (bf16[1,2,256,256]{3,2,1,0:T(8,128)(2,1)S(1)}, bf16[1,2,256,256]{3,2,1,0:T(8,128)(2,1)}, u32[]{:S(2)}) copy-start(bf16[1,2,256,256]{3,2,1,0:T(8,128)(2,1)} %param.7) | copy-start | bytes 786436
  2.3 1.2 copy-start
  2.3 1.5 %copy-start.1 = (bf16[4,1,2,256,256]{4,3,2,1,0:T(8,128)(2,1)S(1)}, bf16[4,1,2,256,256]{4,3,2,1,0:T(8,128)(2,1)}, u32[]{:S(2)}) copy-start(bf16[4,1,2,256,256]{4,3,2,1,0:T(8,128)(2,1)} %gg_ref.1) | copy-start | bytes 3145732
